TPU v7x, 512 devices: a whole 4x4x16 slice. The times are simulated.
512 devices in a mesh: pm: 2 (over y_lo), ka: 128 (over x, z, core), isdf: 2 (over y_hi).
Axes of the slice: x: 4, y: 4 (y_hi: 2, y_lo: 2; y = y_hi * 2 + y_lo), z: 16, core: 2. Of those that a mesh axis runs over, the one named last changes fastest.
Arguments:
- amplitudes: bfloat16 [2, 2, 2, 256, 64, 256], P('pm', None, None, 'ka'), may hold values from -6 to 6
- conduction: bfloat16 [2, 256, 256, 512], P(None, 'ka', None, 'isdf'), may hold values from -0.375 to 0.375
- valence: bfloat16 [2, 256, 64, 512], P(None, 'ka'), may hold values from -0.75 to 0.75
- energy: float32 [256, 64, 256], P('ka', None, 'isdf'), may hold values from 0.5 to 2.5
- screened: bfloat16 [4, 2, 512, 512], P(None, None, 'isdf'), may hold values from -0.59765625 to 0.59765625
- coulomb: float32 [512, 512], P(None, 'isdf'), may hold values from -0.03125 to 0.03125
- mirror: int32 [256], P('ka'), may hold values from 0 to 255, as said below
- transfer_class: int32 [256, 256], P('ka'), may hold values from 0 to 3, as said below
Outputs:
- response: bfloat16 [2, 2, 2, 256, 64, 256], P('pm', None, None, 'ka', None, 'isdf')
Inputs may be any that keep to these rules, and one draw needn't show every extreme that they name: mirror[mirror[k]] = k; a k-point of block j (the aligned block of 2 k-points that holds it) has its mirror in block 127 - j. transfer_class[k, k2] depends only on (k - k2) mod 256.
All inputs are finite; a program needn't handle non-finite values.
Results may differ from a plain program's by a relative error of at most 0.015.
Values may be sent and summed in bfloat16 or wider, within the bound.
A program may use at most 128 MiB of HBM per device.

v0:
```python
import jax
import jax.numpy as jnp
from jax import lax
from jax.sharding import PartitionSpec as P

REACH = 2
HIGHEST = lax.Precision.HIGHEST


def swapped(block, axis, apart):
    count = lax.axis_size(axis)
    route = []
    for low in range(count):
        high = low | 1 << apart
        if high != low and high < count:
            route += [(low, high), (high, low)]
    return lax.ppermute(block, axis, route)


def shifted(value, axis, by):
    size = lax.axis_size(axis)
    return lax.ppermute(value, axis, [(i, (i + by) % size) for i in range(size)])


def pair_einsum(pattern, left, right, conjugate):

    def single(first, second):
        return jnp.einsum(pattern, first, second, preferred_element_type=jnp.float32)

    if conjugate:
        real_part = single(left[0], right[0]) + single(left[1], right[1])
        imag_part = single(left[1], right[0]) - single(left[0], right[1])
    else:
        real_part = single(left[0], right[0]) - single(left[1], right[1])
        imag_part = single(left[0], right[1]) + single(left[1], right[0])
    return (real_part, imag_part)


def conjugated(field):
    return jnp.stack([field[:, 0], -field[:, 1]], axis=1)


def coefficients(vector, conduction):
    real_part, imag_part = pair_einsum(
        "bkvc,kcm->bkvm", (vector[:, 0], vector[:, 1]), (conduction[0], conduction[1]), False
    )
    return jnp.stack([real_part, imag_part], axis=1).astype(jnp.bfloat16)


def amp_bits(field):
    for bit_number in range(lax.axis_size("ka").bit_length() - 1):
        field = swapped(field, "ka", bit_number)
    return field


def result_bits(field):
    for bit_number in range(lax.axis_size("ka").bit_length() - 1):
        field = swapped(field, "ka", bit_number)
    return field


def per_device(amplitudes, conduction, valence, energy, screened, coulomb, mirror, transfer_class):
    pm_index = lax.axis_index("pm")
    ka_index = lax.axis_index("ka")
    isdf_index = lax.axis_index("isdf")
    ka_count = lax.axis_size("ka")
    kpoint_count = conduction.shape[1]
    mu_count = conduction.shape[3]
    point_count = valence.shape[3]
    cond_share = energy.shape[2]
    vector_count = amplitudes.shape[1]
    is_plus = pm_index == 0
    parity = jnp.where(is_plus, 1.0, -1.0).astype(jnp.float32)
    exchange_weight = jnp.where(is_plus, 4.0, 0.0).astype(jnp.float32)
    local_amps = amplitudes[0]
    partner_amps = swapped(local_amps, "pm", 0)
    partner_side = jnp.where(is_plus, partner_amps, local_amps)
    distant_side = amp_bits(partner_side)
    direct = jnp.where(is_plus, local_amps, partner_amps).astype(jnp.float32)
    local_mirror = mirror - (ka_count - 1 - ka_index) * kpoint_count
    flipped = conjugated(jnp.take(distant_side, local_mirror, axis=2).astype(jnp.float32))
    vector = (direct + parity * flipped).astype(jnp.bfloat16)
    own_coef = coefficients(vector, conduction)
    valence_part = lax.dynamic_slice_in_dim(valence, isdf_index * mu_count, mu_count, 3)
    rho_real = jnp.einsum(
        "kvm,bkvm->bm", valence_part[0], own_coef[:, 0], preferred_element_type=jnp.float32
    )
    rho_real = rho_real + jnp.einsum(
        "kvm,bkvm->bm", valence_part[1], own_coef[:, 1], preferred_element_type=jnp.float32
    )
    rho_imag = jnp.einsum(
        "kvm,bkvm->bm", valence_part[0], own_coef[:, 1], preferred_element_type=jnp.float32
    )
    rho_imag = rho_imag - jnp.einsum(
        "kvm,bkvm->bm", valence_part[1], own_coef[:, 0], preferred_element_type=jnp.float32
    )
    density = jnp.stack([rho_real, rho_imag], axis=1)
    spread = jnp.einsum("nm,brm->brn", coulomb, density, precision=HIGHEST)
    spread = lax.psum(spread, ("ka", "isdf"))
    potential = lax.dynamic_slice_in_dim(spread, isdf_index * mu_count, mu_count, 2)
    class_ids = jnp.arange(screened.shape[0], dtype=jnp.int32)

    def accumulate(totals, coef_block, valence_block, source):
        pair_real, pair_imag = pair_einsum(
            "bqvm,qvn->bqmn",
            (coef_block[:, 0], coef_block[:, 1]),
            (valence_block[0], valence_block[1]),
            True,
        )
        pair_real = pair_real.astype(jnp.bfloat16)
        pair_imag = pair_imag.astype(jnp.bfloat16)
        classes = lax.dynamic_slice_in_dim(transfer_class, source * kpoint_count, kpoint_count, 1)
        selector = (classes[:, :, None] == class_ids).astype(jnp.bfloat16)
        total_real, total_imag = totals
        for visitor in range(kpoint_count):
            chosen = jnp.einsum(
                "kw,wrmn->rkmn", selector[:, visitor], screened, preferred_element_type=jnp.float32
            ).astype(jnp.bfloat16)
            screen_real = chosen[0][None].astype(jnp.float32)
            screen_imag = chosen[1][None].astype(jnp.float32)
            visit_real = pair_real[:, visitor][:, None].astype(jnp.float32)
            visit_imag = pair_imag[:, visitor][:, None].astype(jnp.float32)
            total_real = total_real + (screen_real * visit_real - screen_imag * visit_imag)
            total_imag = total_imag + (screen_real * visit_imag + screen_imag * visit_real)
        return (total_real, total_imag)

    payload = (vector, conduction, valence)

    def advance(moving, offset):
        return shifted((moving[0], moving[1], moving[2]), "ka", offset)

    def unpack(moving):
        return (coefficients(moving[0], moving[1]), moving[2])

    def visit(totals, moving, distance):
        coef_block, valence_block = unpack(moving)
        source = jnp.mod(ka_index + distance, ka_count)
        return accumulate(totals, coef_block, valence_block, source)

    zero_field = jnp.zeros((vector_count, kpoint_count, mu_count, point_count), jnp.float32)
    totals = accumulate((zero_field, zero_field), own_coef, valence, ka_index)
    below_item = payload
    for count_done in range(REACH):
        below_item = advance(below_item, 1)
        totals = visit(totals, below_item, -(count_done + 1))
    above_item = payload
    for count_done in range(REACH):
        above_item = advance(above_item, -1)
        totals = visit(totals, above_item, count_done + 1)
    sum_real = totals[0].astype(jnp.bfloat16)
    sum_imag = totals[1].astype(jnp.bfloat16)
    back_real, back_imag = pair_einsum(
        "bkmn,kvn->bkvm", (sum_real, sum_imag), (valence[0], valence[1]), False
    )
    potential_real = potential[:, 0][:, None, None, :]
    potential_imag = potential[:, 1][:, None, None, :]
    exchange_real = potential_real * valence_part[0] - potential_imag * valence_part[1]
    exchange_imag = potential_real * valence_part[1] + potential_imag * valence_part[0]
    field_real = (exchange_weight * exchange_real - back_real).astype(jnp.bfloat16)
    field_imag = (exchange_weight * exchange_imag - back_imag).astype(jnp.bfloat16)
    out_real, out_imag = pair_einsum(
        "bkvm,kcm->bkvc", (field_real, field_imag), (conduction[0], conduction[1]), True
    )
    partial_out = jnp.stack([out_real, out_imag], axis=1)
    summed = lax.psum_scatter(
        partial_out.astype(jnp.bfloat16), "isdf", scatter_dimension=4, tiled=True
    ).astype(jnp.float32)
    vector_part = lax.dynamic_slice_in_dim(vector, isdf_index * cond_share, cond_share, 4).astype(
        jnp.float32
    )
    channel_out = (energy[None, None] * vector_part + summed).astype(jnp.bfloat16)
    partner_out = swapped(channel_out, "pm", 0)
    blended = (
        0.5 * (partner_out.astype(jnp.float32) + parity * channel_out.astype(jnp.float32))
    ).astype(jnp.bfloat16)
    distant_out = result_bits(blended)
    reflected = conjugated(jnp.take(distant_out, local_mirror, axis=2))
    result = jnp.where(is_plus, blended, reflected)
    return result[None]


def solution(mesh):
    return jax.shard_map(
        per_device,
        mesh=mesh,
        in_specs=(
            P("pm", None, None, "ka", None, None),
            P(None, "ka", None, "isdf"),
            P(None, "ka", None, None),
            P("ka", None, "isdf"),
            P(None, None, "isdf", None),
            P(None, "isdf"),
            P("ka"),
            P("ka", None),
        ),
        out_specs=P("pm", None, None, "ka", None, "isdf"),
        check_vma=False,
    )
```

profile of v0, /device:TPU:2, one launch (start us, length us, event | category | flops | bytes accessed | tf_op | source)
XLA Modules:
  0.0 1090.2 jit_solution(7875653439164302398)
XLA Ops:
  8.6 10.8 collective-permute-start.15
  21.3 5.8 collective-permute-start.16
  76.7 6.6 collective-permute-done.2
  87.2 12.3 %collective-permute-done.3 = bf16[2,2,2,64,256]{4,3,0,2,1:T(8,128)(2,1)S(1)} collective-permute-done((bf16[2,2,2,64,256]{4,3,0,2,1:T(8,128)(2,1)S(1)}, bf16[2,2,2,64,256]{4,3,0,2,1:T(8,128)(2,1)S(1)}, u32[]{:S(2)}, u32[]{:S(2)}) %collective-permute-start.3) | collective-permute-done | bytes 262176 | tf_op jit(solution)/shard_map/ppermute | solution.py:17
  104.0 22.7 %collective-permute-done.4 = bf16[2,2,2,64,256]{4,3,0,2,1:T(8,128)(2,1)S(1)} collective-permute-done((bf16[2,2,2,64,256]{4,3,0,2,1:T(8,128)(2,1)S(1)}, bf16[2,2,2,64,256]{4,3,0,2,1:T(8,128)(2,1)S(1)}, u32[]{:S(2)}, u32[]{:S(2)}) %collective-permute-start.4) | collective-permute-done | bytes 262176 | tf_op jit(solution)/shard_map/ppermute | solution.py:17
  126.6 14.7 %collective-permute-start.5 = (bf16[2,2,2,64,256]{4,3,0,2,1:T(8,128)(2,1)S(1)}, bf16[2,2,2,64,256]{4,3,0,2,1:T(8,128)(2,1)S(1)}, u32[]{:S(2)}, u32[]{:S(2)}) collective-permute-start(bf16[2,2,2,64,256]{4,3,0,2,1:T(8,128)(2,1)S(1)} %collective-permute-done.4), channel_id=1, source_target_pairs={{0,32},{32,0},{2,34},{34,2},{4,36},{36,4},{6,38},{38,6},{8,40},{40... | collective-permute-start | bytes 786440 | tf_op jit(solution)/shard_map/ppermute | solution.py:17
  143.4 14.8 %collective-permute-done.5 = bf16[2,2,2,64,256]{4,3,0,2,1:T(8,128)(2,1)S(1)} collective-permute-done((bf16[2,2,2,64,256]{4,3,0,2,1:T(8,128)(2,1)S(1)}, bf16[2,2,2,64,256]{4,3,0,2,1:T(8,128)(2,1)S(1)}, u32[]{:S(2)}, u32[]{:S(2)}) %collective-permute-start.5) | collective-permute-done | bytes 262176 | tf_op jit(solution)/shard_map/ppermute | solution.py:17
  163.1 5.4 collective-permute-done.6
  198.8 5.8 collective-permute-start.19
  206.5 5.8 collective-permute-start.18
  228.5 583.0 %psum.7 = f32[2,2,512]{2,1,0:T(2,128)S(1)} all-reduce(f32[2,2,512]{2,1,0:T(2,128)S(1)} %fusion.90), channel_id=1, replica_groups=mesh['pm'=2,'ka'=128,'isdf'=2] {'ka','isdf'}, use_global_device_ids=true, to_apply=%region_0.1 | all-reduce | flops 2048 | bytes 16384 | tf_op jit(solution)/shard_map/psum | solution.py:99
  845.6 5.3 collective-permute-start.17
  878.6 9.2 add_convert_fusion
  887.9 9.5 add_convert_fusion.1
  901.8 92.5 %reduce-scatter.4.cloned.1.call-done = bf16[128,512]{1,0:T(8,128)(2,1)} async-done(((bf16[256,512]{1,0:T(8,128)(2,1)}), bf16[128,512]{1,0:T(8,128)(2,1)}) %reduce-scatter.4.cloned.1.call-update) | async-done | bytes 131088
  999.0 4.7 collective-permute-done.20
  1014.4 4.4 collective-permute-start.23
  1018.9 5.9 collective-permute-done.23
  1024.7 7.6 collective-permute-start.24
  1032.4 9.9 collective-permute-done.24
  1042.2 12.0 %collective-permute-start.25 = (bf16[2,2,2,64,128]{4,3,0,2,1:T(8,128)(2,1)S(1)}, bf16[2,2,2,64,128]{4,3,0,2,1:T(8,128)(2,1)S(1)}, u32[]{:S(2)}, u32[]{:S(2)}) collective-permute-start(bf16[2,2,2,64,128]{4,3,0,2,1:T(8,128)(2,1)S(1)} %collective-permute-done.24), channel_id=1, source_target_pairs={{0,32},{32,0},{2,34},{34,2},{4,36},{36,4},{6,38},{38,6},{8,40},{40... | collective-permute-start | bytes 393224 | tf_op jit(solution)/shard_map/ppermute | solution.py:17
  1054.2 12.1 %collective-permute-done.25 = bf16[2,2,2,64,128]{4,3,0,2,1:T(8,128)(2,1)S(1)} collective-permute-done((bf16[2,2,2,64,128]{4,3,0,2,1:T(8,128)(2,1)S(1)}, bf16[2,2,2,64,128]{4,3,0,2,1:T(8,128)(2,1)S(1)}, u32[]{:S(2)}, u32[]{:S(2)}) %collective-permute-start.25) | collective-permute-done | bytes 131104 | tf_op jit(solution)/shard_map/ppermute | solution.py:17
  1068.8 4.4 collective-permute-done.26
  1077.1 4.4 collective-permute-done.27
  (293 shorter events, 205.7 us)
Async XLA Ops:
  6.5 987.7 %reduce-scatter.4.cloned.1.call-start = ((), (), s32[]{:S(2)}) async-start(), calls=%async_computation.1 | async-start | bytes 393216
  6.5 198.1 %collective-permute-start.9 = (bf16[2,2,256,256]{3,2,1,0:T(8,128)(2,1)}, bf16[2,2,256,256]{3,2,1,0:T(8,128)(2,1)}, u32[]{:S(2)}, u32[]{:S(2)}) collective-permute-start(bf16[2,2,256,256]{3,2,1,0:T(8,128)(2,1)} %param.9), channel_id=1, source_target_pairs={{0,2},{2,4},{4,6},{6,8},{8,10},{10,12},{12,14},{14,16},{16,18},{18... | collective-permute-start | bytes 1572872 | tf_op jit(solution)/shard_map/ppermute | solution.py:22
  8.6 197.9 %collective-permute-start.15 = (bf16[2,2,256,256]{3,2,1,0:T(8,128)(2,1)}, bf16[2,2,256,256]{3,2,1,0:T(8,128)(2,1)}, u32[]{:S(2)}, u32[]{:S(2)}) collective-permute-start(bf16[2,2,256,256]{3,2,1,0:T(8,128)(2,1)} %param.9), channel_id=1, source_target_pairs={{0,254},{2,0},{4,2},{6,4},{8,6},{10,8},{12,10},{14,12},{16,14},{18... | collective-permute-start | bytes 1572872 | tf_op jit(solution)/shard_map/ppermute | solution.py:22
  19.4 177.4 %collective-permute-start.10 = (bf16[2,2,64,512]{3,2,1,0:T(8,128)(2,1)}, bf16[2,2,64,512]{3,2,1,0:T(8,128)(2,1)}, u32[]{:S(2)}, u32[]{:S(2)}) collective-permute-start(bf16[2,2,64,512]{3,2,1,0:T(8,128)(2,1)} %param.10), channel_id=1, source_target_pairs={{0,2},{2,4},{4,6},{6,8},{8,10},{10,12},{12,14},{14,16},{16,18},{18... | collective-permute-start | bytes 786440 | tf_op jit(solution)/shard_map/ppermute | solution.py:22
  21.3 177.5 %collective-permute-start.16 = (bf16[2,2,64,512]{3,2,1,0:T(8,128)(2,1)}, bf16[2,2,64,512]{3,2,1,0:T(8,128)(2,1)}, u32[]{:S(2)}, u32[]{:S(2)}) collective-permute-start(bf16[2,2,64,512]{3,2,1,0:T(8,128)(2,1)} %param.10), channel_id=1, source_target_pairs={{0,254},{2,0},{4,2},{6,4},{8,6},{10,8},{12,10},{14,12},{16,14},{18... | collective-permute-start | bytes 786440 | tf_op jit(solution)/shard_map/ppermute | solution.py:22
  28.1 40.2 %collective-permute-start = (bf16[2,2,2,64,256]{4,3,0,2,1:T(8,128)(2,1)S(1)}, bf16[2,2,2,64,256]{4,3,0,2,1:T(8,128)(2,1)S(1)}, u32[]{:S(2)}, u32[]{:S(2)}) collective-permute-start(bf16[2,2,2,64,256]{4,3,0,2,1:T(8,128)(2,1)S(1)} %bitcast.651), channel_id=1, source_target_pairs={{0,256},{256,0},{1,257},{257,1},{2,258},{258,2},{3,259},{259,3},{4... | collective-permute-start | bytes 786440 | tf_op jit(solution)/shard_map/ppermute | solution.py:17
  72.5 10.7 collective-permute-start.2
  83.2 16.3 %collective-permute-start.3 = (bf16[2,2,2,64,256]{4,3,0,2,1:T(8,128)(2,1)S(1)}, bf16[2,2,2,64,256]{4,3,0,2,1:T(8,128)(2,1)S(1)}, u32[]{:S(2)}, u32[]{:S(2)}) collective-permute-start(bf16[2,2,2,64,256]{4,3,0,2,1:T(8,128)(2,1)S(1)} %collective-permute-done.2), channel_id=1, source_target_pairs={{0,8},{8,0},{2,10},{10,2},{4,12},{12,4},{6,14},{14,6},{16,24},{24,... | collective-permute-start | bytes 786440 | tf_op jit(solution)/shard_map/ppermute | solution.py:17
  99.5 27.1 %collective-permute-start.4 = (bf16[2,2,2,64,256]{4,3,0,2,1:T(8,128)(2,1)S(1)}, bf16[2,2,2,64,256]{4,3,0,2,1:T(8,128)(2,1)S(1)}, u32[]{:S(2)}, u32[]{:S(2)}) collective-permute-start(bf16[2,2,2,64,256]{4,3,0,2,1:T(8,128)(2,1)S(1)} %collective-permute-done.3), channel_id=1, source_target_pairs={{0,16},{16,0},{2,18},{18,2},{4,20},{20,4},{6,22},{22,6},{8,24},{24... | collective-permute-start | bytes 786440 | tf_op jit(solution)/shard_map/ppermute | solution.py:17
  126.6 31.6 %collective-permute-start.5 = (bf16[2,2,2,64,256]{4,3,0,2,1:T(8,128)(2,1)S(1)}, bf16[2,2,2,64,256]{4,3,0,2,1:T(8,128)(2,1)S(1)}, u32[]{:S(2)}, u32[]{:S(2)}) collective-permute-start(bf16[2,2,2,64,256]{4,3,0,2,1:T(8,128)(2,1)S(1)} %collective-permute-done.4), channel_id=1, source_target_pairs={{0,32},{32,0},{2,34},{34,2},{4,36},{36,4},{6,38},{38,6},{8,40},{40... | collective-permute-start | bytes 786440 | tf_op jit(solution)/shard_map/ppermute | solution.py:17
  158.2 10.2 collective-permute-start.6
  168.4 43.9 %collective-permute-start.7 = (bf16[2,2,2,64,256]{4,3,0,2,1:T(8,128)(2,1)}, bf16[2,2,2,64,256]{4,3,0,2,1:T(8,128)(2,1)}, u32[]{:S(2)}, u32[]{:S(2)}) collective-permute-start(bf16[2,2,2,64,256]{4,3,0,2,1:T(8,128)(2,1)} %collective-permute-done.6), channel_id=1, source_target_pairs={{0,128},{128,0},{2,130},{130,2},{4,132},{132,4},{6,134},{134,6},{8... | collective-permute-start | bytes 786440 | tf_op jit(solution)/shard_map/ppermute | solution.py:17
  196.8 658.7 %collective-permute-start.13 = (bf16[2,2,64,512]{3,2,1,0:T(8,128)(2,1)}, bf16[2,2,64,512]{3,2,1,0:T(8,128)(2,1)}, u32[]{:S(2)}, u32[]{:S(2)}) collective-permute-start(bf16[2,2,64,512]{3,2,1,0:T(8,128)(2,1)} %collective-permute-done.10), channel_id=1, source_target_pairs={{0,2},{2,4},{4,6},{6,8},{8,10},{10,12},{12,14},{14,16},{16,18},{18... | collective-permute-start | bytes 786440 | tf_op jit(solution)/shard_map/ppermute | solution.py:22
  198.8 669.1 %collective-permute-start.19 = (bf16[2,2,64,512]{3,2,1,0:T(8,128)(2,1)}, bf16[2,2,64,512]{3,2,1,0:T(8,128)(2,1)}, u32[]{:S(2)}, u32[]{:S(2)}) collective-permute-start(bf16[2,2,64,512]{3,2,1,0:T(8,128)(2,1)} %collective-permute-done.16), channel_id=1, source_target_pairs={{0,254},{2,0},{4,2},{6,4},{8,6},{10,8},{12,10},{14,12},{16,14},{18... | collective-permute-start | bytes 786440 | tf_op jit(solution)/shard_map/ppermute | solution.py:22
  204.6 641.0 %collective-permute-start.12 = (bf16[2,2,256,256]{3,2,1,0:T(8,128)(2,1)}, bf16[2,2,256,256]{3,2,1,0:T(8,128)(2,1)}, u32[]{:S(2)}, u32[]{:S(2)}) collective-permute-start(bf16[2,2,256,256]{3,2,1,0:T(8,128)(2,1)} %collective-permute-done.9), channel_id=1, source_target_pairs={{0,2},{2,4},{4,6},{6,8},{8,10},{10,12},{12,14},{14,16},{16,18},{18... | collective-permute-start | bytes 1572872 | tf_op jit(solution)/shard_map/ppermute | solution.py:22
  206.5 656.7 %collective-permute-start.18 = (bf16[2,2,256,256]{3,2,1,0:T(8,128)(2,1)}, bf16[2,2,256,256]{3,2,1,0:T(8,128)(2,1)}, u32[]{:S(2)}, u32[]{:S(2)}) collective-permute-start(bf16[2,2,256,256]{3,2,1,0:T(8,128)(2,1)} %collective-permute-done.15), channel_id=1, source_target_pairs={{0,254},{2,0},{4,2},{6,4},{8,6},{10,8},{12,10},{14,12},{16,14},{18... | collective-permute-start | bytes 1572872 | tf_op jit(solution)/shard_map/ppermute | solution.py:22
  221.3 594.7 %collective-permute-start.8 = (bf16[2,2,2,64,256]{4,3,0,2,1:T(8,128)(2,1)}, bf16[2,2,2,64,256]{4,3,0,2,1:T(8,128)(2,1)}, u32[]{:S(2)}, u32[]{:S(2)}) collective-permute-start(bf16[2,2,2,64,256]{4,3,0,2,1:T(8,128)(2,1)} %fusion.89), channel_id=1, source_target_pairs={{0,2},{2,4},{4,6},{6,8},{8,10},{10,12},{12,14},{14,16},{16,18},{18... | collective-permute-start | bytes 786440 | tf_op jit(solution)/shard_map/ppermute | solution.py:22
  816.0 14.6 %collective-permute-start.14 = (bf16[2,2,2,64,256]{4,3,0,2,1:T(8,128)(2,1)}, bf16[2,2,2,64,256]{4,3,0,2,1:T(8,128)(2,1)S(1)}, u32[]{:S(2)}, u32[]{:S(2)}) collective-permute-start(bf16[2,2,2,64,256]{4,3,0,2,1:T(8,128)(2,1)} %fusion.89), channel_id=1, source_target_pairs={{0,254},{2,0},{4,2},{6,4},{8,6},{10,8},{12,10},{14,12},{16,14},{18... | collective-permute-start | bytes 786440 | tf_op jit(solution)/shard_map/ppermute | solution.py:22
  830.6 20.3 %collective-permute-start.11 = (bf16[2,2,2,64,256]{4,3,0,2,1:T(8,128)(2,1)}, bf16[2,2,2,64,256]{4,3,0,2,1:T(8,128)(2,1)S(1)}, u32[]{:S(2)}, u32[]{:S(2)}) collective-permute-start(bf16[2,2,2,64,256]{4,3,0,2,1:T(8,128)(2,1)} %collective-permute-done.8), channel_id=1, source_target_pairs={{0,2},{2,4},{4,6},{6,8},{8,10},{10,12},{12,14},{14,16},{16,18},{18... | collective-permute-start | bytes 786440 | tf_op jit(solution)/shard_map/ppermute | solution.py:22
  845.6 17.6 %collective-permute-start.17 = (bf16[2,2,2,64,256]{4,3,0,2,1:T(8,128)(2,1)S(1)}, bf16[2,2,2,64,256]{4,3,0,2,1:T(8,128)(2,1)S(1)}, u32[]{:S(2)}, u32[]{:S(2)}) collective-permute-start(bf16[2,2,2,64,256]{4,3,0,2,1:T(8,128)(2,1)S(1)} %collective-permute-done.14), channel_id=1, source_target_pairs={{0,254},{2,0},{4,2},{6,4},{8,6},{10,8},{12,10},{14,12},{16,14},{18... | collective-permute-start | bytes 786440 | tf_op jit(solution)/shard_map/ppermute | solution.py:22
  1014.4 10.3 collective-permute-start.23
  1024.7 17.5 %collective-permute-start.24 = (bf16[2,2,2,64,128]{4,3,0,2,1:T(8,128)(2,1)S(1)}, bf16[2,2,2,64,128]{4,3,0,2,1:T(8,128)(2,1)S(1)}, u32[]{:S(2)}, u32[]{:S(2)}) collective-permute-start(bf16[2,2,2,64,128]{4,3,0,2,1:T(8,128)(2,1)S(1)} %collective-permute-done.23), channel_id=1, source_target_pairs={{0,16},{16,0},{2,18},{18,2},{4,20},{20,4},{6,22},{22,6},{8,24},{24... | collective-permute-start | bytes 393224 | tf_op jit(solution)/shard_map/ppermute | solution.py:17
  1042.2 24.1 %collective-permute-start.25 = (bf16[2,2,2,64,128]{4,3,0,2,1:T(8,128)(2,1)S(1)}, bf16[2,2,2,64,128]{4,3,0,2,1:T(8,128)(2,1)S(1)}, u32[]{:S(2)}, u32[]{:S(2)}) collective-permute-start(bf16[2,2,2,64,128]{4,3,0,2,1:T(8,128)(2,1)S(1)} %collective-permute-done.24), channel_id=1, source_target_pairs={{0,32},{32,0},{2,34},{34,2},{4,36},{36,4},{6,38},{38,6},{8,40},{40... | collective-permute-start | bytes 393224 | tf_op jit(solution)/shard_map/ppermute | solution.py:17
  1073.2 8.4 collective-permute-start.27
  (65 other events, 1564.9 us)
Sparse Core Ops, SparseCore 0:
  901.9 92.3 reduce-scatter.3
where the time goes:
time: 1100 us; the launch traced here: 1090 us
  blocking collectives  583 us (53%)
  waiting for transfers between devices  201 us (18%)
  starting transfers between devices  120 us (11%)
  matrix products  76.2 us (7%)
  other arithmetic  56.5 us (5%)
  local copies, waits for them, and re-layouts  38.9 us (4%)
  between operations  15.1 us (1%)
    psum x1, blocking collectives, per_device(): spread = lax.psum(spread, ('ka', 'isdf'))  583 us
    ppermute x16, waiting for transfers between devices, swapped(): return lax.ppermute(block, axis, route)  108 us
    unnamed x2, waiting for transfers between devices  92.5 us
    ppermute x16, starting transfers between devices, swapped(): return lax.ppermute(block, axis, route)  71.8 us
    dot_general x48, matrix products, single(): jnp.einsum(pattern, first, second, preferred_element_type=jnp.float32)  53.3 us
    ppermute x12, starting transfers between devices, shifted(): lax.ppermute(value, axis, [(i, (i + by) % size) for i in range(size)])  47.7 us
    dot_general x10, matrix products, accumulate(): jnp.einsum('kw,wrmn->rkmn', selector[:, visitor], screened, preferred_ele...  22.4 us
  transfers between devices with their start and end apart: 29, of which 14 were waited for; matrix products, arithmetic and copies ran while one was open for 12% of the time, Pallas kernels for 0%

commit v1 on v0

--- a/solution.py
+++ b/solution.py
@@ -5,6 +5,11 @@
 
 REACH = 2
 HIGHEST = lax.Precision.HIGHEST
+
+
+def summed_here(x, axis):
+    parts = lax.all_gather(x, axis)
+    return jnp.sum(parts, axis=0)
 
 
 def swapped(block, axis, apart):
@@ -96,7 +101,7 @@
     )
     density = jnp.stack([rho_real, rho_imag], axis=1)
     spread = jnp.einsum("nm,brm->brn", coulomb, density, precision=HIGHEST)
-    spread = lax.psum(spread, ("ka", "isdf"))
+    spread = summed_here(spread, ("ka", "isdf"))
     potential = lax.dynamic_slice_in_dim(spread, isdf_index * mu_count, mu_count, 2)
     class_ids = jnp.arange(screened.shape[0], dtype=jnp.int32)
 

time: 1100 us -> 553 us (0.50)
  blocking collectives: 583 us -> 0 us
  waiting for transfers between devices: 201 us -> 227 us
    psum x1 -> x0, blocking collectives: 583 us -> none  [per_device(): spread = lax.psum(spread, ('ka', 'isdf'))]
    all_gather x0 -> x1, waiting for transfers between devices: none -> 99.4 us  [summed_here(): parts = lax.all_gather(x, axis)]
    unnamed x2 -> x3, waiting for transfers between devices: 92.5 us -> 18.7 us
  transfers between devices with their start and end apart: 29 -> 30, of which waited for: 14 -> 15; matrix products, arithmetic and copies ran while one was open for 12% -> 31% of each run, Pallas kernels for 0% -> 0%
where the time goes in v1:
time: 553 us; the launch traced here: 542 us
  waiting for transfers between devices  227 us (41%)
  starting transfers between devices  123 us (22%)
  matrix products  78.7 us (14%)
  other arithmetic  58.7 us (11%)
  local copies, waits for them, and re-layouts  39.5 us (7%)
  between operations  15.1 us (3%)
    ppermute x16, waiting for transfers between devices, swapped(): return lax.ppermute(block, axis, route)  108 us
    all_gather x1, waiting for transfers between devices, summed_here(): parts = lax.all_gather(x, axis)  99.4 us
    ppermute x16, starting transfers between devices, swapped(): return lax.ppermute(block, axis, route)  71.7 us
    dot_general x48, matrix products, single(): jnp.einsum(pattern, first, second, preferred_element_type=jnp.float32)  54.8 us
    ppermute x12, starting transfers between devices, shifted(): lax.ppermute(value, axis, [(i, (i + by) % size) for i in range(size)])  51.5 us
    dot_general x10, matrix products, accumulate(): jnp.einsum('kw,wrmn->rkmn', selector[:, visitor], screened, preferred_ele...  22.8 us
    mul x10, other arithmetic, accumulate(): screen_real * visit_real - screen_imag * visit_imag  21.5 us
    unnamed x3, waiting for transfers between devices  18.7 us
  transfers between devices with their start and end apart: 30, of which 15 were waited for; matrix products, arithmetic and copies ran while one was open for 31% of the time, Pallas kernels for 0%

profile of v1, /device:TPU:2, one launch (start us, length us, event | category | flops | bytes accessed | tf_op | source)
XLA Modules:
  0.0 541.9 jit_solution(15929999312341073955)
XLA Ops:
  8.6 10.8 %collective-permute-start.15 = (bf16[2,2,256,256]{3,2,1,0:T(8,128)(2,1)}, bf16[2,2,256,256]{3,2,1,0:T(8,128)(2,1)}, u32[]{:S(2)}, u32[]{:S(2)}) collective-permute-start(bf16[2,2,256,256]{3,2,1,0:T(8,128)(2,1)} %param.9), channel_id=1, source_target_pairs={{0,254},{2,0},{4,2},{6,4},{8,6},{10,8},{12,10},{14,12},{16,14},{18... | collective-permute-start | bytes 1572872 | tf_op jit(solution)/shard_map/ppermute | solution.py:27
  21.3 5.8 %collective-permute-start.16 = (bf16[2,2,64,512]{3,2,1,0:T(8,128)(2,1)}, bf16[2,2,64,512]{3,2,1,0:T(8,128)(2,1)}, u32[]{:S(2)}, u32[]{:S(2)}) collective-permute-start(bf16[2,2,64,512]{3,2,1,0:T(8,128)(2,1)} %param.10), channel_id=1, source_target_pairs={{0,254},{2,0},{4,2},{6,4},{8,6},{10,8},{12,10},{14,12},{16,14},{18... | collective-permute-start | bytes 786440 | tf_op jit(solution)/shard_map/ppermute | solution.py:27
  77.7 6.6 %collective-permute-done.2 = bf16[2,2,2,64,256]{4,3,0,2,1:T(8,128)(2,1)S(1)} collective-permute-done((bf16[2,2,2,64,256]{4,3,0,2,1:T(8,128)(2,1)S(1)}, bf16[2,2,2,64,256]{4,3,0,2,1:T(8,128)(2,1)S(1)}, u32[]{:S(2)}, u32[]{:S(2)}) %collective-permute-start.2) | collective-permute-done | bytes 262176 | tf_op jit(solution)/shard_map/ppermute | solution.py:22
  88.3 12.3 %collective-permute-done.3 = bf16[2,2,2,64,256]{4,3,0,2,1:T(8,128)(2,1)S(1)} collective-permute-done((bf16[2,2,2,64,256]{4,3,0,2,1:T(8,128)(2,1)S(1)}, bf16[2,2,2,64,256]{4,3,0,2,1:T(8,128)(2,1)S(1)}, u32[]{:S(2)}, u32[]{:S(2)}) %collective-permute-start.3) | collective-permute-done | bytes 262176 | tf_op jit(solution)/shard_map/ppermute | solution.py:22
  105.1 22.7 %collective-permute-done.4 = bf16[2,2,2,64,256]{4,3,0,2,1:T(8,128)(2,1)S(1)} collective-permute-done((bf16[2,2,2,64,256]{4,3,0,2,1:T(8,128)(2,1)S(1)}, bf16[2,2,2,64,256]{4,3,0,2,1:T(8,128)(2,1)S(1)}, u32[]{:S(2)}, u32[]{:S(2)}) %collective-permute-start.4) | collective-permute-done | bytes 262176 | tf_op jit(solution)/shard_map/ppermute | solution.py:22
  127.7 14.7 %collective-permute-start.5 = (bf16[2,2,2,64,256]{4,3,0,2,1:T(8,128)(2,1)S(1)}, bf16[2,2,2,64,256]{4,3,0,2,1:T(8,128)(2,1)S(1)}, u32[]{:S(2)}, u32[]{:S(2)}) collective-permute-start(bf16[2,2,2,64,256]{4,3,0,2,1:T(8,128)(2,1)S(1)} %collective-permute-done.4), channel_id=1, source_target_pairs={{0,32},{32,0},{2,34},{34,2},{4,36},{36,4},{6,38},{38,6},{8,40},{40... | collective-permute-start | bytes 786440 | tf_op jit(solution)/shard_map/ppermute | solution.py:22
  144.4 14.9 %collective-permute-done.5 = bf16[2,2,2,64,256]{4,3,0,2,1:T(8,128)(2,1)S(1)} collective-permute-done((bf16[2,2,2,64,256]{4,3,0,2,1:T(8,128)(2,1)S(1)}, bf16[2,2,2,64,256]{4,3,0,2,1:T(8,128)(2,1)S(1)}, u32[]{:S(2)}, u32[]{:S(2)}) %collective-permute-start.5) | collective-permute-done | bytes 262176 | tf_op jit(solution)/shard_map/ppermute | solution.py:22
  164.1 5.4 collective-permute-done.6
  199.7 5.8 %collective-permute-start.19 = (bf16[2,2,64,512]{3,2,1,0:T(8,128)(2,1)}, bf16[2,2,64,512]{3,2,1,0:T(8,128)(2,1)}, u32[]{:S(2)}, u32[]{:S(2)}) collective-permute-start(bf16[2,2,64,512]{3,2,1,0:T(8,128)(2,1)} %collective-permute-done.16), channel_id=1, source_target_pairs={{0,254},{2,0},{4,2},{6,4},{8,6},{10,8},{12,10},{14,12},{16,14},{18... | collective-permute-start | bytes 786440 | tf_op jit(solution)/shard_map/ppermute | solution.py:27
  207.5 5.8 %collective-permute-start.18 = (bf16[2,2,256,256]{3,2,1,0:T(8,128)(2,1)}, bf16[2,2,256,256]{3,2,1,0:T(8,128)(2,1)}, u32[]{:S(2)}, u32[]{:S(2)}) collective-permute-start(bf16[2,2,256,256]{3,2,1,0:T(8,128)(2,1)} %collective-permute-done.15), channel_id=1, source_target_pairs={{0,254},{2,0},{4,2},{6,4},{8,6},{10,8},{12,10},{14,12},{16,14},{18... | collective-permute-start | bytes 1572872 | tf_op jit(solution)/shard_map/ppermute | solution.py:27
  234.6 5.8 %collective-permute-start.14 = (bf16[2,2,2,64,256]{4,3,0,2,1:T(8,128)(2,1)}, bf16[2,2,2,64,256]{4,3,0,2,1:T(8,128)(2,1)S(1)}, u32[]{:S(2)}, u32[]{:S(2)}) collective-permute-start(bf16[2,2,2,64,256]{4,3,0,2,1:T(8,128)(2,1)} %fusion.89), channel_id=1, source_target_pairs={{0,254},{2,0},{4,2},{6,4},{8,6},{10,8},{12,10},{14,12},{16,14},{18... | collective-permute-start | bytes 786440 | tf_op jit(solution)/shard_map/ppermute | solution.py:27
  267.5 6.0 %collective-permute-start.17 = (bf16[2,2,2,64,256]{4,3,0,2,1:T(8,128)(2,1)S(1)}, bf16[2,2,2,64,256]{4,3,0,2,1:T(8,128)(2,1)S(1)}, u32[]{:S(2)}, u32[]{:S(2)}) collective-permute-start(bf16[2,2,2,64,256]{4,3,0,2,1:T(8,128)(2,1)S(1)} %collective-permute-done.14), channel_id=1, source_target_pairs={{0,254},{2,0},{4,2},{6,4},{8,6},{10,8},{12,10},{14,12},{16,14},{18... | collective-permute-start | bytes 786440 | tf_op jit(solution)/shard_map/ppermute | solution.py:27
  301.2 9.3 %add_convert_fusion.1 = bf16[2,2,256,512]{3,2,0,1:T(8,128)(2,1)S(1)} fusion(f32[2,256,512]{2,1,0:T(8,128)} %get-tuple-element.48, f32[2,256,512]{2,1,0:T(8,128)S(1)} %copy-done.14, f32[2,256,512]{2,1,0:T(8,128)} %get-tuple-element.69, f32[2,256,512]{2,1,0:T(8,128)S(1)} %copy-done.13, f32[2,256,512]{2,1,0:T(8,128)} %get-tuple-element.47, ...), kind=kLoop, calls=%fused_computation.3 | loop fusion | flops 20971520 | bytes 42991616 | tf_op jit(solution)/shard_map/convert_element_type | solution.py:155
  312.7 9.5 %add_convert_fusion = bf16[2,2,256,512]{3,2,0,1:T(8,128)(2,1)S(1)} fusion(f32[2,256,512]{2,1,0:T(8,128)} %get-tuple-element.48, f32[2,256,512]{2,1,0:T(8,128)S(1)} %copy-done.14, f32[2,256,512]{2,1,0:T(8,128)} %get-tuple-element.69, f32[2,256,512]{2,1,0:T(8,128)S(1)} %copy-done.13, f32[2,256,512]{2,1,0:T(8,128)} %get-tuple-element.47, ...), kind=kLoop, calls=%fused_computation.2 | loop fusion | flops 20971520 | bytes 42991616 | tf_op jit(solution)/shard_map/convert_element_type | solution.py:156
  322.2 99.4 %all-gather.3.cloned.1.call-done = f32[512,2,512]{2,1,0:T(2,128)} async-done(((f32[2,2,512]{2,1,0:T(2,128)}), f32[512,2,512]{2,1,0:T(2,128)}) %all-gather.3.cloned.1.call-update) | async-done | bytes 2097168 | tf_op jit(solution)/shard_map/all_gather | solution.py:11
  427.3 18.7 %reduce-scatter.4.cloned.1.call-done = bf16[128,512]{1,0:T(8,128)(2,1)} async-done(((bf16[256,512]{1,0:T(8,128)(2,1)}), bf16[128,512]{1,0:T(8,128)(2,1)}) %reduce-scatter.4.cloned.1.call-update) | async-done | bytes 131088
  450.8 4.6 collective-permute-done.20
  466.2 4.4 collective-permute-start.23
  470.6 5.9 %collective-permute-done.23 = bf16[2,2,2,64,128]{4,3,0,2,1:T(8,128)(2,1)S(1)} collective-permute-done((bf16[2,2,2,64,128]{4,3,0,2,1:T(8,128)(2,1)S(1)}, bf16[2,2,2,64,128]{4,3,0,2,1:T(8,128)(2,1)S(1)}, u32[]{:S(2)}, u32[]{:S(2)}) %collective-permute-start.23) | collective-permute-done | bytes 131104 | tf_op jit(solution)/shard_map/ppermute | solution.py:22
  476.5 7.6 %collective-permute-start.24 = (bf16[2,2,2,64,128]{4,3,0,2,1:T(8,128)(2,1)S(1)}, bf16[2,2,2,64,128]{4,3,0,2,1:T(8,128)(2,1)S(1)}, u32[]{:S(2)}, u32[]{:S(2)}) collective-permute-start(bf16[2,2,2,64,128]{4,3,0,2,1:T(8,128)(2,1)S(1)} %collective-permute-done.23), channel_id=1, source_target_pairs={{0,16},{16,0},{2,18},{18,2},{4,20},{20,4},{6,22},{22,6},{8,24},{24... | collective-permute-start | bytes 393224 | tf_op jit(solution)/shard_map/ppermute | solution.py:22
  484.1 9.9 %collective-permute-done.24 = bf16[2,2,2,64,128]{4,3,0,2,1:T(8,128)(2,1)S(1)} collective-permute-done((bf16[2,2,2,64,128]{4,3,0,2,1:T(8,128)(2,1)S(1)}, bf16[2,2,2,64,128]{4,3,0,2,1:T(8,128)(2,1)S(1)}, u32[]{:S(2)}, u32[]{:S(2)}) %collective-permute-start.24) | collective-permute-done | bytes 131104 | tf_op jit(solution)/shard_map/ppermute | solution.py:22
  494.0 12.0 %collective-permute-start.25 = (bf16[2,2,2,64,128]{4,3,0,2,1:T(8,128)(2,1)S(1)}, bf16[2,2,2,64,128]{4,3,0,2,1:T(8,128)(2,1)S(1)}, u32[]{:S(2)}, u32[]{:S(2)}) collective-permute-start(bf16[2,2,2,64,128]{4,3,0,2,1:T(8,128)(2,1)S(1)} %collective-permute-done.24), channel_id=1, source_target_pairs={{0,32},{32,0},{2,34},{34,2},{4,36},{36,4},{6,38},{38,6},{8,40},{40... | collective-permute-start | bytes 393224 | tf_op jit(solution)/shard_map/ppermute | solution.py:22
  506.0 12.1 %collective-permute-done.25 = bf16[2,2,2,64,128]{4,3,0,2,1:T(8,128)(2,1)S(1)} collective-permute-done((bf16[2,2,2,64,128]{4,3,0,2,1:T(8,128)(2,1)S(1)}, bf16[2,2,2,64,128]{4,3,0,2,1:T(8,128)(2,1)S(1)}, u32[]{:S(2)}, u32[]{:S(2)}) %collective-permute-start.25) | collective-permute-done | bytes 131104 | tf_op jit(solution)/shard_map/ppermute | solution.py:22
  520.4 4.5 collective-permute-done.26
  (302 shorter events, 212.7 us)
Async XLA Ops:
  6.5 415.1 %all-gather.3.cloned.1.call-start = ((), (), s32[]{:S(2)}) async-start(), calls=%async_computation.1 | async-start | bytes 2105344 | tf_op jit(solution)/shard_map/all_gather | solution.py:11
  6.5 199.0 %collective-permute-start.9 = (bf16[2,2,256,256]{3,2,1,0:T(8,128)(2,1)}, bf16[2,2,256,256]{3,2,1,0:T(8,128)(2,1)}, u32[]{:S(2)}, u32[]{:S(2)}) collective-permute-start(bf16[2,2,256,256]{3,2,1,0:T(8,128)(2,1)} %param.9), channel_id=1, source_target_pairs={{0,2},{2,4},{4,6},{6,8},{8,10},{10,12},{12,14},{14,16},{16,18},{18... | collective-permute-start | bytes 1572872 | tf_op jit(solution)/shard_map/ppermute | solution.py:27
  8.6 198.9 %collective-permute-start.15 = (bf16[2,2,256,256]{3,2,1,0:T(8,128)(2,1)}, bf16[2,2,256,256]{3,2,1,0:T(8,128)(2,1)}, u32[]{:S(2)}, u32[]{:S(2)}) collective-permute-start(bf16[2,2,256,256]{3,2,1,0:T(8,128)(2,1)} %param.9), channel_id=1, source_target_pairs={{0,254},{2,0},{4,2},{6,4},{8,6},{10,8},{12,10},{14,12},{16,14},{18... | collective-permute-start | bytes 1572872 | tf_op jit(solution)/shard_map/ppermute | solution.py:27
  19.4 178.3 %collective-permute-start.10 = (bf16[2,2,64,512]{3,2,1,0:T(8,128)(2,1)}, bf16[2,2,64,512]{3,2,1,0:T(8,128)(2,1)}, u32[]{:S(2)}, u32[]{:S(2)}) collective-permute-start(bf16[2,2,64,512]{3,2,1,0:T(8,128)(2,1)} %param.10), channel_id=1, source_target_pairs={{0,2},{2,4},{4,6},{6,8},{8,10},{10,12},{12,14},{14,16},{16,18},{18... | collective-permute-start | bytes 786440 | tf_op jit(solution)/shard_map/ppermute | solution.py:27
  21.3 178.4 %collective-permute-start.16 = (bf16[2,2,64,512]{3,2,1,0:T(8,128)(2,1)}, bf16[2,2,64,512]{3,2,1,0:T(8,128)(2,1)}, u32[]{:S(2)}, u32[]{:S(2)}) collective-permute-start(bf16[2,2,64,512]{3,2,1,0:T(8,128)(2,1)} %param.10), channel_id=1, source_target_pairs={{0,254},{2,0},{4,2},{6,4},{8,6},{10,8},{12,10},{14,12},{16,14},{18... | collective-permute-start | bytes 786440 | tf_op jit(solution)/shard_map/ppermute | solution.py:27
  28.8 40.6 %collective-permute-start = (bf16[2,2,2,64,256]{4,3,0,2,1:T(8,128)(2,1)}, bf16[2,2,2,64,256]{4,3,0,2,1:T(8,128)(2,1)S(1)}, u32[]{:S(2)}, u32[]{:S(2)}) collective-permute-start(bf16[2,2,2,64,256]{4,3,0,2,1:T(8,128)(2,1)} %bitcast.647), channel_id=1, source_target_pairs={{0,256},{256,0},{1,257},{257,1},{2,258},{258,2},{3,259},{259,3},{4... | collective-permute-start | bytes 786440 | tf_op jit(solution)/shard_map/ppermute | solution.py:22
  73.6 10.7 %collective-permute-start.2 = (bf16[2,2,2,64,256]{4,3,0,2,1:T(8,128)(2,1)S(1)}, bf16[2,2,2,64,256]{4,3,0,2,1:T(8,128)(2,1)S(1)}, u32[]{:S(2)}, u32[]{:S(2)}) collective-permute-start(bf16[2,2,2,64,256]{4,3,0,2,1:T(8,128)(2,1)S(1)} %collective-permute-done.1), channel_id=1, source_target_pairs={{0,4},{4,0},{2,6},{6,2},{8,12},{12,8},{10,14},{14,10},{16,20},{20,... | collective-permute-start | bytes 786440 | tf_op jit(solution)/shard_map/ppermute | solution.py:22
  84.3 16.3 %collective-permute-start.3 = (bf16[2,2,2,64,256]{4,3,0,2,1:T(8,128)(2,1)S(1)}, bf16[2,2,2,64,256]{4,3,0,2,1:T(8,128)(2,1)S(1)}, u32[]{:S(2)}, u32[]{:S(2)}) collective-permute-start(bf16[2,2,2,64,256]{4,3,0,2,1:T(8,128)(2,1)S(1)} %collective-permute-done.2), channel_id=1, source_target_pairs={{0,8},{8,0},{2,10},{10,2},{4,12},{12,4},{6,14},{14,6},{16,24},{24,... | collective-permute-start | bytes 786440 | tf_op jit(solution)/shard_map/ppermute | solution.py:22
  100.6 27.1 %collective-permute-start.4 = (bf16[2,2,2,64,256]{4,3,0,2,1:T(8,128)(2,1)S(1)}, bf16[2,2,2,64,256]{4,3,0,2,1:T(8,128)(2,1)S(1)}, u32[]{:S(2)}, u32[]{:S(2)}) collective-permute-start(bf16[2,2,2,64,256]{4,3,0,2,1:T(8,128)(2,1)S(1)} %collective-permute-done.3), channel_id=1, source_target_pairs={{0,16},{16,0},{2,18},{18,2},{4,20},{20,4},{6,22},{22,6},{8,24},{24... | collective-permute-start | bytes 786440 | tf_op jit(solution)/shard_map/ppermute | solution.py:22
  127.7 31.6 %collective-permute-start.5 = (bf16[2,2,2,64,256]{4,3,0,2,1:T(8,128)(2,1)S(1)}, bf16[2,2,2,64,256]{4,3,0,2,1:T(8,128)(2,1)S(1)}, u32[]{:S(2)}, u32[]{:S(2)}) collective-permute-start(bf16[2,2,2,64,256]{4,3,0,2,1:T(8,128)(2,1)S(1)} %collective-permute-done.4), channel_id=1, source_target_pairs={{0,32},{32,0},{2,34},{34,2},{4,36},{36,4},{6,38},{38,6},{8,40},{40... | collective-permute-start | bytes 786440 | tf_op jit(solution)/shard_map/ppermute | solution.py:22
  159.3 10.2 %collective-permute-start.6 = (bf16[2,2,2,64,256]{4,3,0,2,1:T(8,128)(2,1)S(1)}, bf16[2,2,2,64,256]{4,3,0,2,1:T(8,128)(2,1)}, u32[]{:S(2)}, u32[]{:S(2)}) collective-permute-start(bf16[2,2,2,64,256]{4,3,0,2,1:T(8,128)(2,1)S(1)} %collective-permute-done.5), channel_id=1, source_target_pairs={{0,64},{64,0},{2,66},{66,2},{4,68},{68,4},{6,70},{70,6},{8,72},{72... | collective-permute-start | bytes 786440 | tf_op jit(solution)/shard_map/ppermute | solution.py:22
  169.5 43.7 %collective-permute-start.7 = (bf16[2,2,2,64,256]{4,3,0,2,1:T(8,128)(2,1)}, bf16[2,2,2,64,256]{4,3,0,2,1:T(8,128)(2,1)}, u32[]{:S(2)}, u32[]{:S(2)}) collective-permute-start(bf16[2,2,2,64,256]{4,3,0,2,1:T(8,128)(2,1)} %collective-permute-done.6), channel_id=1, source_target_pairs={{0,128},{128,0},{2,130},{130,2},{4,132},{132,4},{6,134},{134,6},{8... | collective-permute-start | bytes 786440 | tf_op jit(solution)/shard_map/ppermute | solution.py:22
  197.7 80.4 %collective-permute-start.13 = (bf16[2,2,64,512]{3,2,1,0:T(8,128)(2,1)}, bf16[2,2,64,512]{3,2,1,0:T(8,128)(2,1)}, u32[]{:S(2)}, u32[]{:S(2)}) collective-permute-start(bf16[2,2,64,512]{3,2,1,0:T(8,128)(2,1)} %collective-permute-done.10), channel_id=1, source_target_pairs={{0,2},{2,4},{4,6},{6,8},{8,10},{10,12},{12,14},{14,16},{16,18},{18... | collective-permute-start | bytes 786440 | tf_op jit(solution)/shard_map/ppermute | solution.py:27
  199.7 90.8 %collective-permute-start.19 = (bf16[2,2,64,512]{3,2,1,0:T(8,128)(2,1)}, bf16[2,2,64,512]{3,2,1,0:T(8,128)(2,1)}, u32[]{:S(2)}, u32[]{:S(2)}) collective-permute-start(bf16[2,2,64,512]{3,2,1,0:T(8,128)(2,1)} %collective-permute-done.16), channel_id=1, source_target_pairs={{0,254},{2,0},{4,2},{6,4},{8,6},{10,8},{12,10},{14,12},{16,14},{18... | collective-permute-start | bytes 786440 | tf_op jit(solution)/shard_map/ppermute | solution.py:27
  205.5 62.0 %collective-permute-start.12 = (bf16[2,2,256,256]{3,2,1,0:T(8,128)(2,1)}, bf16[2,2,256,256]{3,2,1,0:T(8,128)(2,1)}, u32[]{:S(2)}, u32[]{:S(2)}) collective-permute-start(bf16[2,2,256,256]{3,2,1,0:T(8,128)(2,1)} %collective-permute-done.9), channel_id=1, source_target_pairs={{0,2},{2,4},{4,6},{6,8},{8,10},{10,12},{12,14},{14,16},{16,18},{18... | collective-permute-start | bytes 1572872 | tf_op jit(solution)/shard_map/ppermute | solution.py:27
  207.5 78.4 %collective-permute-start.18 = (bf16[2,2,256,256]{3,2,1,0:T(8,128)(2,1)}, bf16[2,2,256,256]{3,2,1,0:T(8,128)(2,1)}, u32[]{:S(2)}, u32[]{:S(2)}) collective-permute-start(bf16[2,2,256,256]{3,2,1,0:T(8,128)(2,1)} %collective-permute-done.15), channel_id=1, source_target_pairs={{0,254},{2,0},{4,2},{6,4},{8,6},{10,8},{12,10},{14,12},{16,14},{18... | collective-permute-start | bytes 1572872 | tf_op jit(solution)/shard_map/ppermute | solution.py:27
  222.2 12.4 %collective-permute-start.8 = (bf16[2,2,2,64,256]{4,3,0,2,1:T(8,128)(2,1)}, bf16[2,2,2,64,256]{4,3,0,2,1:T(8,128)(2,1)}, u32[]{:S(2)}, u32[]{:S(2)}) collective-permute-start(bf16[2,2,2,64,256]{4,3,0,2,1:T(8,128)(2,1)} %fusion.89), channel_id=1, source_target_pairs={{0,2},{2,4},{4,6},{6,8},{8,10},{10,12},{12,14},{14,16},{16,18},{18... | collective-permute-start | bytes 786440 | tf_op jit(solution)/shard_map/ppermute | solution.py:27
  230.1 216.0 %reduce-scatter.4.cloned.1.call-start = ((), (), s32[]{:S(2)}) async-start(), calls=%async_computation.2 | async-start | bytes 393216
  234.6 18.5 %collective-permute-start.14 = (bf16[2,2,2,64,256]{4,3,0,2,1:T(8,128)(2,1)}, bf16[2,2,2,64,256]{4,3,0,2,1:T(8,128)(2,1)S(1)}, u32[]{:S(2)}, u32[]{:S(2)}) collective-permute-start(bf16[2,2,2,64,256]{4,3,0,2,1:T(8,128)(2,1)} %fusion.89), channel_id=1, source_target_pairs={{0,254},{2,0},{4,2},{6,4},{8,6},{10,8},{12,10},{14,12},{16,14},{18... | collective-permute-start | bytes 786440 | tf_op jit(solution)/shard_map/ppermute | solution.py:27
  253.1 20.4 %collective-permute-start.11 = (bf16[2,2,2,64,256]{4,3,0,2,1:T(8,128)(2,1)}, bf16[2,2,2,64,256]{4,3,0,2,1:T(8,128)(2,1)S(1)}, u32[]{:S(2)}, u32[]{:S(2)}) collective-permute-start(bf16[2,2,2,64,256]{4,3,0,2,1:T(8,128)(2,1)} %collective-permute-done.8), channel_id=1, source_target_pairs={{0,2},{2,4},{4,6},{6,8},{8,10},{10,12},{12,14},{14,16},{16,18},{18... | collective-permute-start | bytes 786440 | tf_op jit(solution)/shard_map/ppermute | solution.py:27
  267.5 18.3 %collective-permute-start.17 = (bf16[2,2,2,64,256]{4,3,0,2,1:T(8,128)(2,1)S(1)}, bf16[2,2,2,64,256]{4,3,0,2,1:T(8,128)(2,1)S(1)}, u32[]{:S(2)}, u32[]{:S(2)}) collective-permute-start(bf16[2,2,2,64,256]{4,3,0,2,1:T(8,128)(2,1)S(1)} %collective-permute-done.14), channel_id=1, source_target_pairs={{0,254},{2,0},{4,2},{6,4},{8,6},{10,8},{12,10},{14,12},{16,14},{18... | collective-permute-start | bytes 786440 | tf_op jit(solution)/shard_map/ppermute | solution.py:27
  466.2 10.3 %collective-permute-start.23 = (bf16[2,2,2,64,128]{4,3,0,2,1:T(8,128)(2,1)S(1)}, bf16[2,2,2,64,128]{4,3,0,2,1:T(8,128)(2,1)S(1)}, u32[]{:S(2)}, u32[]{:S(2)}) collective-permute-start(bf16[2,2,2,64,128]{4,3,0,2,1:T(8,128)(2,1)S(1)} %collective-permute-done.22), channel_id=1, source_target_pairs={{0,8},{8,0},{2,10},{10,2},{4,12},{12,4},{6,14},{14,6},{16,24},{24,... | collective-permute-start | bytes 393224 | tf_op jit(solution)/shard_map/ppermute | solution.py:22
  476.5 17.5 %collective-permute-start.24 = (bf16[2,2,2,64,128]{4,3,0,2,1:T(8,128)(2,1)S(1)}, bf16[2,2,2,64,128]{4,3,0,2,1:T(8,128)(2,1)S(1)}, u32[]{:S(2)}, u32[]{:S(2)}) collective-permute-start(bf16[2,2,2,64,128]{4,3,0,2,1:T(8,128)(2,1)S(1)} %collective-permute-done.23), channel_id=1, source_target_pairs={{0,16},{16,0},{2,18},{18,2},{4,20},{20,4},{6,22},{22,6},{8,24},{24... | collective-permute-start | bytes 393224 | tf_op jit(solution)/shard_map/ppermute | solution.py:22
  494.0 24.1 %collective-permute-start.25 = (bf16[2,2,2,64,128]{4,3,0,2,1:T(8,128)(2,1)S(1)}, bf16[2,2,2,64,128]{4,3,0,2,1:T(8,128)(2,1)S(1)}, u32[]{:S(2)}, u32[]{:S(2)}) collective-permute-start(bf16[2,2,2,64,128]{4,3,0,2,1:T(8,128)(2,1)S(1)} %collective-permute-done.24), channel_id=1, source_target_pairs={{0,32},{32,0},{2,34},{34,2},{4,36},{36,4},{6,38},{38,6},{8,40},{40... | collective-permute-start | bytes 393224 | tf_op jit(solution)/shard_map/ppermute | solution.py:22
  (69 other events, 1257.1 us)
Sparse Core Ops, SparseCore 0:
  230.2 191.3 all-gather.2
  427.5 18.5 reduce-scatter.3
